TPU v7x, 32 devices: a whole 2x2x4 slice. The times are simulated.
32 devices in a mesh: ctx: 8 (over y, x, core), grp: 4 (over z).
Axes of the slice: x: 2, y: 2, z: 4, core: 2. Of those that a mesh axis runs over, the one named last changes fastest.
Arguments:
- q_latent: bfloat16 [8, 128, 512], P('grp', 'ctx'), parts along dimension 0, may hold values from -48 to 48
- q_rope: bfloat16 [8, 128, 64], P('grp', 'ctx'), parts along dimension 0, may hold values from -48 to 48
- latent_cache: bfloat16 [256, 64, 576], P(('grp', 'ctx')), parts along dimension 0, may hold values from -6 to 6
- page_table: int32 [8, 32], P('grp'), parts along dimension 0, may hold values from 0 to 63, as said below
- lengths: int32 [8], P('grp'), parts along dimension 0, may hold values from 1 to 2048, 2560 in all
- w_uv: bfloat16 [128, 512, 128], P('ctx'), may hold values from -6 to 6
- w_out: bfloat16 [16384, 7168], P('ctx'), may hold values from -0.046875 to 0.046875
Outputs:
- layer_out: bfloat16 [8, 7168], P('grp'), parts along dimension 0
There are 4 independent parts, one for each index of `grp`. A program takes and returns all parts, laid end to end along the dimension named above; an argument that names none is the same for every part. Nothing has to cross between parts.
Inputs may be any that keep to these rules, and one draw needn't show every extreme that they name: `page_table`: every page number stands exactly once in the table. The longest row is at most 2048; all lengths sum to 2560.
All inputs are finite; a program needn't handle non-finite values.
Results may differ from a plain program's by a relative error of at most 0.03.
Values may be sent and summed in bfloat16 or wider, within the bound.
A program may use at most 128 MiB of HBM per device.

v0:
```python
import jax
import jax.numpy as jnp
from jax import lax
from jax.sharding import PartitionSpec as P

ROPE = 64
V = 128


NEG = -1e30


def finish(row_sums, row_outs, w_uv, w_out):
    latent = (row_outs / row_sums[..., None]).astype(jnp.bfloat16)
    head_out = jnp.einsum("rhc,hcv->rhv", latent, w_uv, preferred_element_type=jnp.float32).astype(
        jnp.bfloat16
    )
    flat = head_out.reshape(head_out.shape[0], -1)
    return jnp.dot(flat, w_out, preferred_element_type=jnp.float32)


def local(q_latent, q_rope, latent_cache, page_table, lengths, w_uv, w_out):
    score_scale = (V + ROPE) ** (-0.5)
    local_query = jnp.concatenate([q_latent, q_rope], axis=2)
    all_query = lax.all_gather(local_query, "ctx", axis=1, tiled=True)
    pages_here = latent_cache.shape[0]
    page_len = latent_cache.shape[1]
    row_count = page_table.shape[0]
    slot_width = page_table.shape[1]
    slot_count = row_count * slot_width
    latent_width = q_latent.shape[2]
    inverse = (
        jnp.zeros((slot_count,), jnp.int32)
        .at[page_table.reshape(-1)]
        .set(jnp.arange(slot_count, dtype=jnp.int32))
    )
    first_page = lax.axis_index("ctx") * pages_here
    slot_ids = lax.dynamic_slice_in_dim(inverse, first_page, pages_here)
    owner_row = slot_ids // slot_width
    logical = slot_ids % slot_width
    page_query = all_query[owner_row]
    scores = (
        jnp.einsum("phc,ptc->pht", page_query, latent_cache, preferred_element_type=jnp.float32)
        * score_scale
    )
    position = logical[:, None] * page_len + jnp.arange(page_len, dtype=jnp.int32)[None, :]
    live_mask = position < lengths[owner_row][:, None]
    scores = jnp.where(live_mask[:, None, :], scores, jnp.float32(NEG))
    page_top = jnp.max(scores, axis=2)
    member = owner_row[None, :] == jnp.arange(row_count, dtype=jnp.int32)[:, None]
    row_top = jnp.max(jnp.where(member[:, :, None], page_top[None, :, :], jnp.float32(NEG)), axis=1)
    row_shift = row_top[owner_row]
    weights = jnp.where(
        live_mask[:, None, :], jnp.exp(scores - row_shift[:, :, None]), jnp.float32(0.0)
    ).astype(jnp.bfloat16)
    page_sum = jnp.sum(weights.astype(jnp.float32), axis=2)
    page_out = jnp.einsum(
        "pht,ptc->phc",
        weights,
        latent_cache[:, :, :latent_width],
        preferred_element_type=jnp.float32,
    )
    onehot = member.astype(jnp.float32)
    row_sum = jnp.dot(onehot, page_sum, precision=lax.Precision.HIGHEST)
    row_out = jnp.dot(
        onehot, page_out.reshape(pages_here, -1), precision=lax.Precision.HIGHEST
    ).reshape(row_count, -1, latent_width)
    tops = lax.all_to_all(
        row_top[None].astype(jnp.bfloat16), "ctx", split_axis=2, concat_axis=0, tiled=True
    ).astype(jnp.float32)
    sums = lax.all_to_all(
        row_sum[None].astype(jnp.bfloat16), "ctx", split_axis=2, concat_axis=0, tiled=True
    ).astype(jnp.float32)
    outs = lax.all_to_all(
        row_out[None].astype(jnp.bfloat16), "ctx", split_axis=2, concat_axis=0, tiled=True
    ).astype(jnp.float32)
    best = jnp.max(tops, axis=0)
    factor = jnp.exp(tops - best[None])
    merged_sum = jnp.sum(factor * sums, axis=0)
    merged_out = jnp.sum(factor[..., None] * outs, axis=0)
    partial_out = finish(merged_sum, merged_out, w_uv, w_out)
    return lax.psum(partial_out, "ctx").astype(jnp.bfloat16)


def solution(mesh):
    in_specs = (
        P("grp", "ctx", None),
        P("grp", "ctx", None),
        P(("grp", "ctx"), None, None),
        P("grp", None),
        P("grp"),
        P("ctx", None, None),
        P("ctx", None),
    )
    out_specs = P("grp", None)
    return jax.shard_map(local, mesh=mesh, in_specs=in_specs, out_specs=out_specs, check_vma=False)
```

profile of v0, /device:TPU:0, one launch (start us, length us, event | category | flops | bytes accessed | tf_op | source)
XLA Modules:
  0.0 82.4 jit_solution(5539018036710012772)
XLA Ops:
  0.0 0.9 %reshape.121 = s32[64,1]{0,1:T(1,128)S(1)} reshape(s32[2,32]{1,0:T(2,128)} %param.10) | data formatting | bytes 512 | tf_op jit(solution)/shard_map/reshape | solution.py:34
  0.9 0.8 scatter_custom_fusion
  1.9 0.8 pad_maximum_fusion
  2.7 11.0 %all_gather.3 = bf16[2,128,576]{2,1,0:T(8,128)(2,1)S(1)} all-gather(bf16[2,16,576]{2,1,0:T(8,128)(2,1)S(1)} %pad_maximum_fusion), channel_id=1, replica_groups=mesh['ctx'=8,'grp'=4] {'ctx'}, dimensions={1}, use_global_device_ids=true | all-gather | bytes 331776 | tf_op jit(solution)/shard_map/all_gather | solution.py:25
  13.7 1.3 %gather_fusion = s32[8]{0:T(128)S(1)} fusion(s32[2]{0:T(128)} %param.11, s32[1024]{0:T(1024)S(1)} %pad_clamp_fusion), kind=kCustom, calls=%fused_computation | custom fusion | bytes 96 | tf_op jit(solution)/shard_map/gather | solution.py:47
  15.0 1.8 %gather_fusion.1 = bf16[8,128,576]{2,1,0:T(8,128)(2,1)} fusion(bf16[2,128,576]{2,1,0:T(8,128)(2,1)S(1)} %all_gather.3, s32[1024]{0:T(1024)S(1)} %pad_clamp_fusion), kind=kCustom, calls=%fused_computation.1 | custom fusion | bytes 2359328 | tf_op jit(solution)/shard_map/gather | solution.py:41
  16.8 2.0 %fusion.17 = (f32[8,128]{1,0:T(8,128)S(1)}, f32[8,128,64]{1,2,0:T(8,128)S(1)}) fusion(bf16[8,128,576]{2,1,0:T(8,128)(2,1)} %gather_fusion.1, bf16[8,64,576]{2,1,0:T(8,128)(2,1)S(1)} %copy-done.1, pred[8,64]{1,0:T(8,128)(4,1)S(1)} %add_compare_fusion), kind=kOutput, calls=%fused_computation.45 | convolution fusion | flops 75693056 | bytes 2036224 | tf_op jit(solution)/shard_map/phc,ptc->pht/dot_general | solution.py:43
  18.9 0.8 copy.37
  19.7 3.3 %all-to-all-start = ((bf16[1,2,128]{1,0,2:T(2,128)(2,1)}), bf16[1,2,128]{1,0,2:T(2,128)(2,1)S(1)}, u32[]{:S(2)}, u32[]{:S(2)}) async-start(bf16[1,2,128]{1,0,2:T(2,128)(2,1)} %copy.37), calls=%async_computation | async-start | bytes 131072 | tf_op jit(solution)/shard_map/all_to_all | solution.py:68
  23.0 0.6 gather_fusion.2
  23.6 0.1 convert_reduce_fusion
  23.7 2.1 %convolution_bitcast_fusion = f32[1,8,128,512]{3,2,1,0:T(8,128)} fusion(bf16[8,64,576]{2,1,0:T(8,128)(2,1)S(1)} %copy-done.1, f32[8,128,64]{1,2,0:T(8,128)S(1)} %get-tuple-element.12, f32[8,128]{1,0:T(8,128)S(1)} %gather_fusion.2, pred[8,64]{1,0:T(8,128)(4,1)S(1)} %add_compare_fusion), kind=kOutput, calls=%fused_computation.4 | convolution fusion | flops 67305472 | bytes 2888704 | tf_op jit(solution)/shard_map/pht,ptc->phc/dot_general | solution.py:57
  25.8 0.1 fusion.3
  25.9 0.8 copy.41
  26.7 1.3 %all-to-all-done = bf16[1,2,128]{1,0,2:T(2,128)(2,1)S(1)} async-done(((bf16[1,2,128]{1,0,2:T(2,128)(2,1)}), bf16[1,2,128]{1,0,2:T(2,128)(2,1)S(1)}, u32[]{:S(2)}, u32[]{:S(2)}) %all-to-all-start) | async-done | bytes 544 | tf_op jit(solution)/shard_map/all_to_all | solution.py:68
  28.0 3.3 %all-to-all-start.2 = ((bf16[1,2,128]{1,0,2:T(2,128)(2,1)}), bf16[1,2,128]{1,0,2:T(2,128)(2,1)S(1)}, u32[]{:S(2)}, u32[]{:S(2)}) async-start(bf16[1,2,128]{1,0,2:T(2,128)(2,1)} %copy.41), calls=%async_computation.2 | async-start | bytes 131072 | tf_op jit(solution)/shard_map/all_to_all | solution.py:71
  31.3 4.5 %fusion = bf16[1,2,128,512]{3,1,0,2:T(2,128)(2,1)} fusion(s32[8]{0:T(128)S(1)} %get-tuple-element.8, f32[1,8,128,512]{3,2,1,0:T(8,128)} %convolution_bitcast_fusion), kind=kOutput, calls=%fused_computation.6 | convolution fusion | flops 12714000 | bytes 2359328 | tf_op jit(solution)/shard_map/dot_general | solution.py:65
  36.0 0.3 all-to-all-done.2
  36.3 3.9 %all-to-all-start.1 = ((bf16[1,2,128,512]{3,1,0,2:T(2,128)(2,1)}), bf16[1,2,128,512]{3,1,0,2:T(2,128)(2,1)S(1)}, u32[]{:S(2)}, u32[]{:S(2)}) async-start(bf16[1,2,128,512]{3,1,0,2:T(2,128)(2,1)} %fusion), calls=%async_computation.1 | async-start | bytes 524288 | tf_op jit(solution)/shard_map/all_to_all | solution.py:74
  40.4 0.1 copy.39
  40.6 6.5 %all-to-all-done.1 = bf16[1,2,128,512]{3,1,0,2:T(2,128)(2,1)S(1)} async-done(((bf16[1,2,128,512]{3,1,0,2:T(2,128)(2,1)}), bf16[1,2,128,512]{3,1,0,2:T(2,128)(2,1)S(1)}, u32[]{:S(2)}, u32[]{:S(2)}) %all-to-all-start.1) | async-done | bytes 262176 | tf_op jit(solution)/shard_map/all_to_all | solution.py:74
  47.1 0.3 fusion.4
  47.5 11.6 %fusion.6 = f32[2,7168]{1,0:T(2,128)S(1)} fusion(bf16[2048,7168]{1,0:T(8,128)(2,1)} %param.13, bf16[16,512,128]{2,1,0:T(8,128)(2,1)S(1)} %copy-done, f32[2,16,512]{2,0,1:T(2,128)S(1)} %fusion.4, f32[2,16]{0,1:T(8,128)S(1)} %copy.43), kind=kOutput, calls=%fused_computation.16 | convolution fusion | flops 62951424 | bytes 31580288 | tf_op jit(solution)/shard_map/dot_general | solution.py:19
  59.0 23.3 %psum.7 = bf16[2,7168]{1,0:T(2,128)(2,1)} all-reduce(f32[2,7168]{1,0:T(2,128)S(1)} %fusion.6), channel_id=1, replica_groups=mesh['ctx'=8,'grp'=4] {'ctx'}, use_global_device_ids=true, to_apply=%region_7.8 | all-reduce | flops 14336 | bytes 86016 | tf_op jit(solution)/shard_map/psum | solution.py:82
  (21 shorter events, 0.8 us)
Async XLA Ops:
  0.0 47.5 %copy-start = (bf16[16,512,128]{2,1,0:T(8,128)(2,1)S(1)}, bf16[16,512,128]{2,1,0:T(8,128)(2,1)}, u32[]{:S(2)}) copy-start(bf16[16,512,128]{2,1,0:T(8,128)(2,1)} %param.12) | copy-start | bytes 6291460
  0.0 16.8 %copy-start.1 = (bf16[8,64,576]{2,1,0:T(8,128)(2,1)S(1)}, bf16[8,64,576]{2,1,0:T(8,128)(2,1)}, u32[]{:S(2)}) copy-start(bf16[8,64,576]{2,1,0:T(8,128)(2,1)} %param.9) | copy-start | bytes 1769476
  19.7 8.3 %all-to-all-start = ((bf16[1,2,128]{1,0,2:T(2,128)(2,1)}), bf16[1,2,128]{1,0,2:T(2,128)(2,1)S(1)}, u32[]{:S(2)}, u32[]{:S(2)}) async-start(bf16[1,2,128]{1,0,2:T(2,128)(2,1)} %copy.37), calls=%async_computation | async-start | bytes 131072 | tf_op jit(solution)/shard_map/all_to_all | solution.py:68
  28.0 8.3 %all-to-all-start.2 = ((bf16[1,2,128]{1,0,2:T(2,128)(2,1)}), bf16[1,2,128]{1,0,2:T(2,128)(2,1)S(1)}, u32[]{:S(2)}, u32[]{:S(2)}) async-start(bf16[1,2,128]{1,0,2:T(2,128)(2,1)} %copy.41), calls=%async_computation.2 | async-start | bytes 131072 | tf_op jit(solution)/shard_map/all_to_all | solution.py:71
  36.3 10.8 %all-to-all-start.1 = ((bf16[1,2,128,512]{3,1,0,2:T(2,128)(2,1)}), bf16[1,2,128,512]{3,1,0,2:T(2,128)(2,1)S(1)}, u32[]{:S(2)}, u32[]{:S(2)}) async-start(bf16[1,2,128,512]{3,1,0,2:T(2,128)(2,1)} %fusion), calls=%async_computation.1 | async-start | bytes 524288 | tf_op jit(solution)/shard_map/all_to_all | solution.py:74
where the time goes:
time: 83 us; the launch traced here: 82.4 us
  blocking collectives  34.4 us (41%)
  matrix products  20.2 us (24%)
  starting transfers between devices  10.6 us (13%)
  waiting for transfers between devices  8.03 us (10%)
  local copies, waits for them, and re-layouts  7.39 us (9%)
  other arithmetic  1.7 us (2%)
    psum x1, blocking collectives, local(): return lax.psum(partial_out, 'ctx').astype(jnp.bfloat16)  23.3 us
    dot_general x1, matrix products, finish(): return jnp.dot(flat, w_out, preferred_element_type=jnp.float32)  11.6 us
    all_gather x1, blocking collectives, local(): all_query = lax.all_gather(local_query, 'ctx', axis=1, tiled=True)  11 us
    all_to_all x1, waiting for transfers between devices, local(): lax.all_to_all(row_out[None].astype(jnp.bfloat16), 'ctx', split_axis=2, c...  6.49 us
    dot_general x1, matrix products, local(): jnp.dot(onehot, page_out.reshape(pages_here, -1), precision=lax.Precision...  4.52 us
    all_to_all x1, starting transfers between devices, local(): lax.all_to_all(row_out[None].astype(jnp.bfloat16), 'ctx', split_axis=2, c...  3.89 us
    all_to_all x1, starting transfers between devices, local(): lax.all_to_all(row_sum[None].astype(jnp.bfloat16), 'ctx', split_axis=2, c...  3.35 us
    all_to_all x1, starting transfers between devices, local(): lax.all_to_all(row_top[None].astype(jnp.bfloat16), 'ctx', split_axis=2, c...  3.35 us
  transfers between devices with their start and end apart: 3, of which 3 were waited for; matrix products, arithmetic and copies ran while one was open for 11% of the time, Pallas kernels for 0%

commit v1 on v0

--- a/solution.py
+++ b/solution.py
@@ -1,6 +1,10 @@
+import functools
+
 import jax
 import jax.numpy as jnp
 from jax import lax
+from jax.experimental import pallas as pl
+from jax.experimental.pallas import tpu as pltpu
 from jax.sharding import PartitionSpec as P
 
 ROPE = 64
@@ -8,6 +12,12 @@
 
 
 NEG = -1e30
+FLOOR = -1e29
+N = 8
+TILE = 1024
+LANES = 128
+GROUPS = ((0, 1), (2, 3), (4, 5), (6, 7))
+SEND_ORDER = (6, 7, 2, 4, 3, 5, 1)
 
 
 def finish(row_sums, row_outs, w_uv, w_out):
@@ -65,12 +75,8 @@
     row_out = jnp.dot(
         onehot, page_out.reshape(pages_here, -1), precision=lax.Precision.HIGHEST
     ).reshape(row_count, -1, latent_width)
-    tops = lax.all_to_all(
-        row_top[None].astype(jnp.bfloat16), "ctx", split_axis=2, concat_axis=0, tiled=True
-    ).astype(jnp.float32)
-    sums = lax.all_to_all(
-        row_sum[None].astype(jnp.bfloat16), "ctx", split_axis=2, concat_axis=0, tiled=True
-    ).astype(jnp.float32)
+    tops = lax.all_to_all(row_top[None], "ctx", split_axis=2, concat_axis=0, tiled=True)
+    sums = lax.all_to_all(row_sum[None], "ctx", split_axis=2, concat_axis=0, tiled=True)
     outs = lax.all_to_all(
         row_out[None].astype(jnp.bfloat16), "ctx", split_axis=2, concat_axis=0, tiled=True
     ).astype(jnp.float32)
@@ -82,6 +88,237 @@
     return lax.psum(partial_out, "ctx").astype(jnp.bfloat16)
 
 
+def partner(me, k):
+    peer = 0
+    for bit in (1, 2, 4):
+        mine = (me // bit) % 2
+        peer = peer + bit * ((1 - mine) if k & bit else mine)
+    return peer
+
+
+def pieces(value, count):
+    terms = []
+    for _ in range(count):
+        term = value.astype(jnp.bfloat16).astype(jnp.float32)
+        terms.append(term)
+        value = value - term
+    return terms
+
+
+def kernel(
+    ql_ref, qr_ref, cache_ref, table_ref, len_ref, uv_ref, wo_ref, out_ref,
+    qall, rope, kv, states, got, uv, wo, part, parts, flat, dense,
+    local_sem, wo_sem, q_send, q_recv, s_send, s_recv, p_send, p_recv,
+):
+    rows, heads, width = ql_ref.shape
+    pages, page_len, key_width = cache_ref.shape
+    tokens = pages * page_len
+    slots = table_ref.shape[1]
+    tiles = wo.shape[0]
+    scale = (V + ROPE) ** (-0.5)
+    me = lax.axis_index("ctx")
+    peers = [partner(me, k) for k in range(N)]
+
+    barrier = pltpu.get_barrier_semaphore()
+    for k in SEND_ORDER:
+        pl.semaphore_signal(
+            barrier, inc=1, device_id={"ctx": peers[k]}, device_id_type=pl.DeviceIdType.MESH
+        )
+
+    load_ql = pltpu.make_async_copy(ql_ref, qall.at[0, :, :, pl.ds(0, width)], local_sem.at[0])
+    load_qr = pltpu.make_async_copy(qr_ref, rope, local_sem.at[1])
+    load_kv = pltpu.make_async_copy(cache_ref, kv, local_sem.at[2])
+    load_uv = pltpu.make_async_copy(uv_ref, uv, local_sem.at[3])
+    load_ql.start()
+    load_qr.start()
+    load_kv.start()
+    load_uv.start()
+
+    def load_wo(j):
+        return pltpu.make_async_copy(
+            wo_ref.at[:, pl.ds(pl.multiple_of(j * TILE, TILE), TILE)], wo.at[j], wo_sem.at[j]
+        )
+
+    for j in range(tiles):
+        load_wo(j).start()
+
+    def remote(src, dst, send, recv, k):
+        return pltpu.make_async_remote_copy(
+            src_ref=src, dst_ref=dst, send_sem=send, recv_sem=recv,
+            device_id={"ctx": peers[k]}, device_id_type=pl.DeviceIdType.MESH,
+        )
+
+    def query_copy(k):
+        return remote(qall.at[0], qall.at[k], q_send.at[k], q_recv.at[k], k)
+
+    def state_copy(k):
+        return remote(states.at[k], got.at[k], s_send.at[k], s_recv.at[k], k)
+
+    load_ql.wait()
+    load_qr.wait()
+    qall[0, :, :, width:] = jnp.concatenate([rope[...], jnp.zeros_like(rope)], axis=2)
+    pl.semaphore_wait(barrier, N - 1)
+    for k in SEND_ORDER:
+        query_copy(k).start()
+
+    lane = lax.broadcasted_iota(jnp.int32, (1, tokens), 1)
+    page = lane // page_len + me * pages
+    offset = lane % page_len
+    live = []
+    for r in range(rows):
+        limit = jnp.zeros((1, tokens), jnp.int32)
+        for j in range(slots):
+            limit = jnp.where(page == table_ref[r, j], len_ref[r] - j * page_len, limit)
+        live.append(offset < limit)
+
+    load_kv.wait()
+    keys = kv[...].reshape(tokens, key_width)
+    block = rows * heads
+    for group in GROUPS:
+        for k in group:
+            if k:
+                query_copy(k).wait_recv()
+        first, count = group[0], len(group)
+        query = qall[first : first + count].reshape(count * block, width + LANES)[:, :key_width]
+        scores = (
+            lax.dot_general(
+                query, keys, (((1,), (1,)), ((), ())), preferred_element_type=jnp.float32
+            )
+            * scale
+        )
+        scores = jnp.concatenate(
+            [
+                jnp.where(live[i % rows], scores[i * heads : (i + 1) * heads], jnp.float32(NEG))
+                for i in range(count * rows)
+            ],
+            axis=0,
+        )
+        top = jnp.max(scores, axis=1, keepdims=True)
+        weights = jnp.exp(scores - jnp.maximum(top, jnp.float32(FLOOR))).astype(jnp.bfloat16)
+        total = jnp.sum(weights.astype(jnp.float32), axis=1, keepdims=True)
+        summed = jnp.dot(weights, keys[:, :width], preferred_element_type=jnp.float32)
+        states[first : first + count, :, :, :width] = summed.astype(jnp.bfloat16).reshape(
+            count, rows, heads, width
+        )
+        place = lax.broadcasted_iota(jnp.int32, (count * block, LANES), 1)
+        stats = jnp.zeros((count * block, LANES), jnp.float32)
+        for i, term in enumerate(pieces(top, 3) + pieces(total, 3)):
+            stats = jnp.where(place == i, term, stats)
+        states[first : first + count, :, :, width:] = stats.astype(jnp.bfloat16).reshape(
+            count, rows, heads, LANES
+        )
+        for k in group:
+            if k:
+                state_copy(k).start()
+
+    place = lax.broadcasted_iota(jnp.int32, (block, LANES), 1)
+    tops, sums = [], []
+    for k in range(N):
+        if k:
+            state_copy(k).wait_recv()
+        source = got.at[k] if k else states.at[0]
+        stats = source[:, :, width:].reshape(block, LANES).astype(jnp.float32)
+        tops.append(jnp.sum(jnp.where(place < 3, stats, 0.0), axis=1, keepdims=True))
+        sums.append(
+            jnp.sum(jnp.where((place >= 3) & (place < 6), stats, 0.0), axis=1, keepdims=True)
+        )
+    best = functools.reduce(jnp.maximum, tops)
+    merged = jnp.zeros((block, width), jnp.float32)
+    merged_sum = jnp.zeros((block, 1), jnp.float32)
+    for k in range(N):
+        source = got.at[k] if k else states.at[0]
+        factor = jnp.exp(tops[k] - best)
+        merged_sum = merged_sum + factor * sums[k]
+        merged = merged + factor * source[:, :, :width].reshape(block, width).astype(jnp.float32)
+    latent = (merged / merged_sum).astype(jnp.bfloat16)
+
+    load_uv.wait()
+    for h in range(0, heads, 2):
+        pair = jnp.concatenate([uv[h], uv[h + 1]], axis=1)
+        product = jnp.dot(latent, pair, preferred_element_type=jnp.float32)
+        for r in range(rows):
+            for i in range(2):
+                row = r * heads + h + i
+                flat[r : r + 1, (h + i) * V : (h + i + 1) * V] = product[
+                    row : row + 1, i * V : (i + 1) * V
+                ]
+    head_out = flat[...].astype(jnp.bfloat16)
+
+    def step(j, carry):
+        load_wo(j).wait()
+        term = jnp.dot(head_out, wo[j], preferred_element_type=jnp.float32)
+        for c in range(TILE // LANES):
+            dense[c * rows : (c + 1) * rows, :] = term[:, c * LANES : (c + 1) * LANES]
+        part[j] = dense[...].astype(jnp.bfloat16)
+        for k in SEND_ORDER:
+            remote(part.at[j], parts.at[k, j], p_send.at[k], p_recv.at[k], k).start()
+        return carry
+
+    lax.fori_loop(0, tiles, step, 0)
+
+    terms = []
+    for k in range(N):
+        if k:
+            remote(part, parts.at[k], p_send.at[k], p_recv.at[k], k).wait_recv()
+        terms.append((parts[k] if k else part[...]).astype(jnp.float32))
+    while len(terms) > 1:
+        terms = [terms[i] + terms[i + 1] for i in range(0, len(terms), 2)]
+    total = terms[0]
+    for j in range(tiles):
+        for c in range(TILE // LANES):
+            start = j * TILE + c * LANES
+            out_ref[:, start : start + LANES] = total[j, c * rows : (c + 1) * rows, :]
+
+    for k in SEND_ORDER:
+        query_copy(k).wait_send()
+        state_copy(k).wait_send()
+        remote(part, parts.at[k], p_send.at[k], p_recv.at[k], k).wait_send()
+
+
+def fused(q_latent, q_rope, latent_cache, page_table, lengths, w_uv, w_out):
+    rows, heads, width = q_latent.shape
+    depth, columns = w_out.shape
+    tiles = columns // TILE
+    dense_rows = TILE // LANES * rows
+    bf16 = jnp.bfloat16
+    any_space = pl.BlockSpec(memory_space=pl.ANY)
+    smem = pl.BlockSpec(memory_space=pltpu.SMEM)
+    out = pl.pallas_call(
+        kernel,
+        out_shape=jax.ShapeDtypeStruct((rows, columns), jnp.float32),
+        in_specs=[any_space, any_space, any_space, smem, smem, any_space, any_space],
+        out_specs=pl.BlockSpec(memory_space=pltpu.VMEM),
+        scratch_shapes=[
+            pltpu.VMEM((N, rows, heads, width + LANES), bf16),
+            pltpu.VMEM(q_rope.shape, bf16),
+            pltpu.VMEM(latent_cache.shape, bf16),
+            pltpu.VMEM((N, rows, heads, width + LANES), bf16),
+            pltpu.VMEM((N, rows, heads, width + LANES), bf16),
+            pltpu.VMEM(w_uv.shape, bf16),
+            pltpu.VMEM((tiles, depth, TILE), bf16),
+            pltpu.VMEM((tiles, dense_rows, LANES), bf16),
+            pltpu.VMEM((N, tiles, dense_rows, LANES), bf16),
+            pltpu.VMEM((rows, depth), jnp.float32),
+            pltpu.VMEM((dense_rows, LANES), jnp.float32),
+            pltpu.SemaphoreType.DMA((4,)),
+            pltpu.SemaphoreType.DMA((tiles,)),
+            pltpu.SemaphoreType.DMA((N,)),
+            pltpu.SemaphoreType.DMA((N,)),
+            pltpu.SemaphoreType.DMA((N,)),
+            pltpu.SemaphoreType.DMA((N,)),
+            pltpu.SemaphoreType.DMA((N,)),
+            pltpu.SemaphoreType.DMA((N,)),
+        ],
+        compiler_params=pltpu.CompilerParams(
+            collective_id=0, has_side_effects=True, vmem_limit_bytes=56 * 1024 * 1024
+        ),
+        cost_estimate=pl.CostEstimate(
+            flops=2 * rows * depth * columns, bytes_accessed=2 * depth * columns, transcendentals=0
+        ),
+    )(q_latent, q_rope, latent_cache, page_table, lengths, w_uv, w_out)
+    return out.astype(bf16)
+
+
 def solution(mesh):
     in_specs = (
         P("grp", "ctx", None),
@@ -93,4 +330,20 @@
         P("ctx", None),
     )
     out_specs = P("grp", None)
-    return jax.shard_map(local, mesh=mesh, in_specs=in_specs, out_specs=out_specs, check_vma=False)
+
+    def program(q_latent, q_rope, latent_cache, page_table, lengths, w_uv, w_out):
+        rows, heads, width = q_latent.shape
+        suits = (
+            mesh.shape["ctx"] == N
+            and rows * (TILE // LANES) == 16
+            and heads % 16 == 0
+            and width % LANES == 0
+            and w_uv.shape[2] == V
+            and w_out.shape[1] % TILE == 0
+            and w_out.size * 2 <= 32 * 1024 * 1024
+            and latent_cache.size * 2 <= 2 * 1024 * 1024
+        )
+        body = fused if suits else local
+        return body(q_latent, q_rope, latent_cache, page_table, lengths, w_uv, w_out)
+
+    return jax.shard_map(program, mesh=mesh, in_specs=in_specs, out_specs=out_specs, check_vma=False)

time: 83 us -> 30.7 us (0.37)
  blocking collectives: 34.4 us -> 0 us
  Pallas kernels: 0 us -> 29.1 us
  matrix products: 20.2 us -> 0 us
  starting transfers between devices: 10.6 us -> 0 us
  waiting for transfers between devices: 8.03 us -> 0 us
  local copies, waits for them, and re-layouts: 7.39 us -> 0 us
    pallas_call x0 -> x1, Pallas kernels: none -> 29.1 us  [fused(): pl.pallas_call(kernel, out_shape=jax.ShapeDtypeStruct((rows, columns), jn...]
    psum x1 -> x0, blocking collectives: 23.3 us -> none  [local(): return lax.psum(partial_out, 'ctx').astype(jnp.bfloat16)]
    dot_general x5 -> x0, matrix products: 20.2 us -> none  [the longest x1 11.6 us: finish(): return jnp.dot(flat, w_out, preferred_element_type=jnp.float32)]
    all_gather x1 -> x0, blocking collectives: 11 us -> none  [local(): all_query = lax.all_gather(local_query, 'ctx', axis=1, tiled=True)]
    all_to_all x3 -> x0, starting transfers between devices: 10.6 us -> none  [the longest x1 3.89 us: local(): lax.all_to_all(row_out[None].astype(jnp.bfloat16), 'ctx', split_axis=2, c...]
    all_to_all x3 -> x0, waiting for transfers between devices: 8.03 us -> none  [the longest x1 6.49 us: local(): lax.all_to_all(row_out[None].astype(jnp.bfloat16), 'ctx', split_axis=2, c...]
    gather x3 -> x0, local copies, waits for them, and re-layouts: 3.63 us -> none  [the longest x1 1.77 us: local(): page_query = all_query[owner_row]]
    convert_element_type x3 -> x0, local copies, waits for them, and re-layouts: 1.61 us -> none  [the longest x1 0.77 us: local(): row_sum[None].astype(jnp.bfloat16)]
  transfers between devices with their start and end apart: 3 -> 0, of which waited for: 3 -> 0; matrix products, arithmetic and copies ran while one was open for 11% -> 0% of each run, Pallas kernels for 0% -> 0%
where the time goes in v1:
time: 30.7 us; the launch traced here: 30.6 us
  Pallas kernels  29.1 us (95%)
  other arithmetic  1.45 us (5%)
    pallas_call x1, Pallas kernels, fused(): pl.pallas_call(kernel, out_shape=jax.ShapeDtypeStruct((rows, columns), jn...  29.1 us
    convert_element_type x1, other arithmetic, fused(): return out.astype(bf16)  1.45 us

profile of v1, /device:TPU:0, one launch (start us, length us, event | category | flops | bytes accessed | tf_op | source)
XLA Modules:
  0.0 30.6 jit_solution(14802951841598223770)
XLA Ops:
  0.0 29.1 %shard_map.73 = f32[2,7168]{1,0:T(2,128)} custom-call(bf16[2,16,512]{2,1,0:T(8,128)(2,1)} %ql_ref.1, bf16[2,16,64]{2,1,0:T(8,128)(2,1)} %qr_ref.1, bf16[8,64,576]{2,1,0:T(8,128)(2,1)} %cache_ref.1, s32[2,32]{1,0:T(2,128)} %table_ref.1, s32[2]{0:T(128)} %len_ref.1, bf16[16,512,128]{2,1,0:T(8,128)(2,1)} %uv_ref.1, bf16[2048,7168]{1,0:T(8,128)(2,1)} %wo_ref.1), custom_call_target="tpu_custom_call" | custom-call | flops 58720256 | bytes 29360128 | tf_op jit(solution)/shard_map/pallas_call | solution.py:286
  29.1 1.4 %convert_element_type.3 = bf16[2,7168]{1,0:T(2,128)(2,1)} convert(f32[2,7168]{1,0:T(2,128)} %shard_map.73) | non-fusion elementwise | flops 14336 | bytes 86016 | tf_op jit(solution)/shard_map/convert_element_type | solution.py:319

commit v2 on v1

--- a/solution.py
+++ b/solution.py
@@ -16,7 +16,9 @@
 N = 8
 TILE = 1024
 LANES = 128
-GROUPS = ((0, 1), (2, 3), (4, 5), (6, 7))
+CHIPS = 4
+GROUPS = ((0, 1), (2, 3))
+CHIP_ORDER = (3, 1, 2)
 SEND_ORDER = (6, 7, 2, 4, 3, 5, 1)
 
 
@@ -106,13 +108,13 @@
 
 
 def kernel(
-    ql_ref, qr_ref, cache_ref, table_ref, len_ref, uv_ref, wo_ref, out_ref,
-    qall, rope, kv, states, got, uv, wo, part, parts, flat, dense,
-    local_sem, wo_sem, q_send, q_recv, s_send, s_recv, p_send, p_recv,
+    ql_ref, qr_ref, cache_ref, table_hbm, len_hbm, uv_ref, wo_ref, out_ref,
+    qall, rope, kv, states, got, uv, wo, part, parts, flat, dense, table_ref, len_ref,
+    local_sem, wo_sem, kv_send, kv_recv, q_send, q_recv, s_send, s_recv, p_send, p_recv,
 ):
     rows, heads, width = ql_ref.shape
     pages, page_len, key_width = cache_ref.shape
-    tokens = pages * page_len
+    tokens = 2 * pages * page_len
     slots = table_ref.shape[1]
     tiles = wo.shape[0]
     scale = (V + ROPE) ** (-0.5)
@@ -127,10 +129,14 @@
 
     load_ql = pltpu.make_async_copy(ql_ref, qall.at[0, :, :, pl.ds(0, width)], local_sem.at[0])
     load_qr = pltpu.make_async_copy(qr_ref, rope, local_sem.at[1])
-    load_kv = pltpu.make_async_copy(cache_ref, kv, local_sem.at[2])
+    load_kv = pltpu.make_async_copy(cache_ref, kv.at[0], local_sem.at[2])
     load_uv = pltpu.make_async_copy(uv_ref, uv, local_sem.at[3])
+    load_table = pltpu.make_async_copy(table_hbm, table_ref, local_sem.at[4])
+    load_len = pltpu.make_async_copy(len_hbm, len_ref, local_sem.at[5])
     load_ql.start()
     load_qr.start()
+    load_table.start()
+    load_len.start()
     load_kv.start()
     load_uv.start()
 
@@ -148,21 +154,27 @@
             device_id={"ctx": peers[k]}, device_id_type=pl.DeviceIdType.MESH,
         )
 
-    def query_copy(k):
-        return remote(qall.at[0], qall.at[k], q_send.at[k], q_recv.at[k], k)
-
-    def state_copy(k):
-        return remote(states.at[k], got.at[k], s_send.at[k], s_recv.at[k], k)
+    def query_copy(e):
+        return remote(qall.at[0], qall.at[e], q_send.at[e], q_recv.at[e], 2 * e)
+
+    def state_copy(e):
+        return remote(states.at[e], got.at[e], s_send.at[e], s_recv.at[e], 2 * e)
+
+    swap = remote(cache_ref, kv.at[1], kv_send, kv_recv, 1)
 
     load_ql.wait()
     load_qr.wait()
     qall[0, :, :, width:] = jnp.concatenate([rope[...], jnp.zeros_like(rope)], axis=2)
     pl.semaphore_wait(barrier, N - 1)
-    for k in SEND_ORDER:
-        query_copy(k).start()
-
+    for e in CHIP_ORDER:
+        query_copy(e).start()
+    swap.start()
+
+    load_table.wait()
+    load_len.wait()
     lane = lax.broadcasted_iota(jnp.int32, (1, tokens), 1)
-    page = lane // page_len + me * pages
+    page = lane // page_len
+    page = jnp.where(page < pages, page + me * pages, page + (peers[1] - 1) * pages)
     offset = lane % page_len
     live = []
     for r in range(rows):
@@ -172,12 +184,13 @@
         live.append(offset < limit)
 
     load_kv.wait()
+    swap.wait_recv()
     keys = kv[...].reshape(tokens, key_width)
     block = rows * heads
     for group in GROUPS:
-        for k in group:
-            if k:
-                query_copy(k).wait_recv()
+        for e in group:
+            if e:
+                query_copy(e).wait_recv()
         first, count = group[0], len(group)
         query = qall[first : first + count].reshape(count * block, width + LANES)[:, :key_width]
         scores = (
@@ -207,16 +220,16 @@
         states[first : first + count, :, :, width:] = stats.astype(jnp.bfloat16).reshape(
             count, rows, heads, LANES
         )
-        for k in group:
-            if k:
-                state_copy(k).start()
+        for e in group:
+            if e:
+                state_copy(e).start()
 
     place = lax.broadcasted_iota(jnp.int32, (block, LANES), 1)
     tops, sums = [], []
-    for k in range(N):
-        if k:
-            state_copy(k).wait_recv()
-        source = got.at[k] if k else states.at[0]
+    for e in range(CHIPS):
+        if e:
+            state_copy(e).wait_recv()
+        source = got.at[e] if e else states.at[0]
         stats = source[:, :, width:].reshape(block, LANES).astype(jnp.float32)
         tops.append(jnp.sum(jnp.where(place < 3, stats, 0.0), axis=1, keepdims=True))
         sums.append(
@@ -225,10 +238,10 @@
     best = functools.reduce(jnp.maximum, tops)
     merged = jnp.zeros((block, width), jnp.float32)
     merged_sum = jnp.zeros((block, 1), jnp.float32)
-    for k in range(N):
-        source = got.at[k] if k else states.at[0]
-        factor = jnp.exp(tops[k] - best)
-        merged_sum = merged_sum + factor * sums[k]
+    for e in range(CHIPS):
+        source = got.at[e] if e else states.at[0]
+        factor = jnp.exp(tops[e] - best)
+        merged_sum = merged_sum + factor * sums[e]
         merged = merged + factor * source[:, :, :width].reshape(block, width).astype(jnp.float32)
     latent = (merged / merged_sum).astype(jnp.bfloat16)
 
@@ -269,9 +282,11 @@
             start = j * TILE + c * LANES
             out_ref[:, start : start + LANES] = total[j, c * rows : (c + 1) * rows, :]
 
+    swap.wait_send()
+    for e in CHIP_ORDER:
+        query_copy(e).wait_send()
+        state_copy(e).wait_send()
     for k in SEND_ORDER:
-        query_copy(k).wait_send()
-        state_copy(k).wait_send()
         remote(part, parts.at[k], p_send.at[k], p_recv.at[k], k).wait_send()
 
 
@@ -282,30 +297,33 @@
     dense_rows = TILE // LANES * rows
     bf16 = jnp.bfloat16
     any_space = pl.BlockSpec(memory_space=pl.ANY)
-    smem = pl.BlockSpec(memory_space=pltpu.SMEM)
     out = pl.pallas_call(
         kernel,
-        out_shape=jax.ShapeDtypeStruct((rows, columns), jnp.float32),
-        in_specs=[any_space, any_space, any_space, smem, smem, any_space, any_space],
+        out_shape=pltpu.VMEM((rows, columns), jnp.float32),
+        in_specs=[any_space] * 7,
         out_specs=pl.BlockSpec(memory_space=pltpu.VMEM),
         scratch_shapes=[
-            pltpu.VMEM((N, rows, heads, width + LANES), bf16),
+            pltpu.VMEM((CHIPS, rows, heads, width + LANES), bf16),
             pltpu.VMEM(q_rope.shape, bf16),
-            pltpu.VMEM(latent_cache.shape, bf16),
-            pltpu.VMEM((N, rows, heads, width + LANES), bf16),
-            pltpu.VMEM((N, rows, heads, width + LANES), bf16),
+            pltpu.VMEM((2,) + latent_cache.shape, bf16),
+            pltpu.VMEM((CHIPS, rows, heads, width + LANES), bf16),
+            pltpu.VMEM((CHIPS, rows, heads, width + LANES), bf16),
             pltpu.VMEM(w_uv.shape, bf16),
             pltpu.VMEM((tiles, depth, TILE), bf16),
             pltpu.VMEM((tiles, dense_rows, LANES), bf16),
             pltpu.VMEM((N, tiles, dense_rows, LANES), bf16),
             pltpu.VMEM((rows, depth), jnp.float32),
             pltpu.VMEM((dense_rows, LANES), jnp.float32),
-            pltpu.SemaphoreType.DMA((4,)),
+            pltpu.SMEM(page_table.shape, jnp.int32),
+            pltpu.SMEM(lengths.shape, jnp.int32),
+            pltpu.SemaphoreType.DMA((6,)),
             pltpu.SemaphoreType.DMA((tiles,)),
-            pltpu.SemaphoreType.DMA((N,)),
-            pltpu.SemaphoreType.DMA((N,)),
-            pltpu.SemaphoreType.DMA((N,)),
-            pltpu.SemaphoreType.DMA((N,)),
+            pltpu.SemaphoreType.DMA,
+            pltpu.SemaphoreType.DMA,
+            pltpu.SemaphoreType.DMA((CHIPS,)),
+            pltpu.SemaphoreType.DMA((CHIPS,)),
+            pltpu.SemaphoreType.DMA((CHIPS,)),
+            pltpu.SemaphoreType.DMA((CHIPS,)),
             pltpu.SemaphoreType.DMA((N,)),
             pltpu.SemaphoreType.DMA((N,)),
         ],

time: 30.7 us -> 25.5 us (0.83)
  Pallas kernels: 29.1 us -> 24.7 us
  other arithmetic: 1.45 us -> 0.63 us
    pallas_call x1, Pallas kernels: 29.1 us -> 24.7 us  [fused(): pl.pallas_call(kernel, out_shape=pltpu.VMEM((rows, columns), jnp.float32)...]
    convert_element_type x1, other arithmetic: 1.45 us -> 0.63 us  [fused(): return out.astype(bf16)]
where the time goes in v2:
time: 25.5 us; the launch traced here: 25.3 us
  Pallas kernels  24.7 us (97%)
  other arithmetic  0.63 us (2%)
    pallas_call x1, Pallas kernels, fused(): pl.pallas_call(kernel, out_shape=pltpu.VMEM((rows, columns), jnp.float32)...  24.7 us
    convert_element_type x1, other arithmetic, fused(): return out.astype(bf16)  0.63 us

profile of v2, /device:TPU:0, one launch (start us, length us, event | category | flops | bytes accessed | tf_op | source)
XLA Modules:
  0.0 25.3 jit_solution(11954192337916149682)
XLA Ops:
  0.0 24.7 %shard_map.73 = f32[2,7168]{1,0:T(2,128)S(1)} custom-call(bf16[2,16,512]{2,1,0:T(8,128)(2,1)} %ql_ref.1, bf16[2,16,64]{2,1,0:T(8,128)(2,1)} %qr_ref.1, bf16[8,64,576]{2,1,0:T(8,128)(2,1)} %cache_ref.1, s32[2,32]{1,0:T(2,128)} %table_hbm.1, s32[2]{0:T(128)} %len_hbm.1, bf16[16,512,128]{2,1,0:T(8,128)(2,1)} %uv_ref.1, bf16[2048,7168]{1,0:T(8,128)(2,1)} %wo_ref.1), custom_call_target="tpu_custom_call" | custom-call | flops 58720256 | bytes 29360128 | tf_op jit(solution)/shard_map/pallas_call | solution.py:300
  24.7 0.6 %convert_element_type.3 = bf16[2,7168]{1,0:T(2,128)(2,1)} convert(f32[2,7168]{1,0:T(2,128)S(1)} %shard_map.73) | non-fusion elementwise | flops 14336 | bytes 86016 | tf_op jit(solution)/shard_map/convert_element_type | solution.py:337

commit v3 on v2

--- a/solution.py
+++ b/solution.py
@@ -17,7 +17,9 @@
 TILE = 1024
 LANES = 128
 CHIPS = 4
-GROUPS = ((0, 1), (2, 3))
+GROUPS = ((1, 2, 3), (0,))
+EARLY = 1
+LATE = 2
 CHIP_ORDER = (3, 1, 2)
 SEND_ORDER = (6, 7, 2, 4, 3, 5, 1)
 
@@ -138,14 +140,13 @@
     load_table.start()
     load_len.start()
     load_kv.start()
-    load_uv.start()
 
     def load_wo(j):
         return pltpu.make_async_copy(
             wo_ref.at[:, pl.ds(pl.multiple_of(j * TILE, TILE), TILE)], wo.at[j], wo_sem.at[j]
         )
 
-    for j in range(tiles):
+    for j in range(EARLY):
         load_wo(j).start()
 
     def remote(src, dst, send, recv, k):
@@ -160,15 +161,19 @@
     def state_copy(e):
         return remote(states.at[e], got.at[e], s_send.at[e], s_recv.at[e], 2 * e)
 
-    swap = remote(cache_ref, kv.at[1], kv_send, kv_recv, 1)
+    swap = remote(kv.at[0], kv.at[1], kv_send, kv_recv, 1)
 
     load_ql.wait()
     load_qr.wait()
     qall[0, :, :, width:] = jnp.concatenate([rope[...], jnp.zeros_like(rope)], axis=2)
+    load_kv.wait()
     pl.semaphore_wait(barrier, N - 1)
+    swap.start()
     for e in CHIP_ORDER:
         query_copy(e).start()
-    swap.start()
+    load_uv.start()
+    for j in range(EARLY, tiles):
+        load_wo(j).start()
 
     load_table.wait()
     load_len.wait()
@@ -183,7 +188,6 @@
             limit = jnp.where(page == table_ref[r, j], len_ref[r] - j * page_len, limit)
         live.append(offset < limit)
 
-    load_kv.wait()
     swap.wait_recv()
     keys = kv[...].reshape(tokens, key_width)
     block = rows * heads
@@ -263,11 +267,13 @@
         for c in range(TILE // LANES):
             dense[c * rows : (c + 1) * rows, :] = term[:, c * LANES : (c + 1) * LANES]
         part[j] = dense[...].astype(jnp.bfloat16)
+        return carry
+
+    for begin, end in ((0, tiles - LATE), (tiles - LATE, tiles)):
+        lax.fori_loop(begin, end, step, 0)
+        some = pl.ds(begin, end - begin)
         for k in SEND_ORDER:
-            remote(part.at[j], parts.at[k, j], p_send.at[k], p_recv.at[k], k).start()
-        return carry
-
-    lax.fori_loop(0, tiles, step, 0)
+            remote(part.at[some], parts.at[k, some], p_send.at[k], p_recv.at[k], k).start()
 
     terms = []
     for k in range(N):
@@ -358,6 +364,7 @@
             and width % LANES == 0
             and w_uv.shape[2] == V
             and w_out.shape[1] % TILE == 0
+            and w_out.shape[1] > LATE * TILE
             and w_out.size * 2 <= 32 * 1024 * 1024
             and latent_cache.size * 2 <= 2 * 1024 * 1024
         )

time: 25.5 us -> 22.5 us (0.88)
  Pallas kernels: 24.7 us -> 21.7 us
    pallas_call x1, Pallas kernels: 24.7 us -> 21.7 us  [fused(): pl.pallas_call(kernel, out_shape=pltpu.VMEM((rows, columns), jnp.float32)...]
where the time goes in v3:
time: 22.5 us; the launch traced here: 22.4 us
  Pallas kernels  21.7 us (96%)
  other arithmetic  0.63 us (3%)
    pallas_call x1, Pallas kernels, fused(): pl.pallas_call(kernel, out_shape=pltpu.VMEM((rows, columns), jnp.float32)...  21.7 us
    convert_element_type x1, other arithmetic, fused(): return out.astype(bf16)  0.63 us

profile of v3, /device:TPU:0, one launch (start us, length us, event | category | flops | bytes accessed | tf_op | source)
XLA Modules:
  0.0 22.4 jit_solution(15368584571404643635)
XLA Ops:
  0.0 21.7 %shard_map.73 = f32[2,7168]{1,0:T(2,128)S(1)} custom-call(bf16[2,16,512]{2,1,0:T(8,128)(2,1)} %ql_ref.1, bf16[2,16,64]{2,1,0:T(8,128)(2,1)} %qr_ref.1, bf16[8,64,576]{2,1,0:T(8,128)(2,1)} %cache_ref.1, s32[2,32]{1,0:T(2,128)} %table_hbm.1, s32[2]{0:T(128)} %len_hbm.1, bf16[16,512,128]{2,1,0:T(8,128)(2,1)} %uv_ref.1, bf16[2048,7168]{1,0:T(8,128)(2,1)} %wo_ref.1), custom_call_target="tpu_custom_call" | custom-call | flops 58720256 | bytes 29360128 | tf_op jit(solution)/shard_map/pallas_call | solution.py:306
  21.7 0.6 %convert_element_type.3 = bf16[2,7168]{1,0:T(2,128)(2,1)} convert(f32[2,7168]{1,0:T(2,128)S(1)} %shard_map.73) | non-fusion elementwise | flops 14336 | bytes 86016 | tf_op jit(solution)/shard_map/convert_element_type | solution.py:343

commit v4 on v3

--- a/solution.py
+++ b/solution.py
@@ -18,7 +18,7 @@
 LANES = 128
 CHIPS = 4
 GROUPS = ((1, 2, 3), (0,))
-EARLY = 1
+EARLY = 3
 LATE = 2
 CHIP_ORDER = (3, 1, 2)
 SEND_ORDER = (6, 7, 2, 4, 3, 5, 1)
@@ -111,7 +111,7 @@
 
 def kernel(
     ql_ref, qr_ref, cache_ref, table_hbm, len_hbm, uv_ref, wo_ref, out_ref,
-    qall, rope, kv, states, got, uv, wo, part, parts, flat, dense, table_ref, len_ref,
+    qall, rope, kv, states, got, uv, wo, part, parts, flat, table_ref, len_ref,
     local_sem, wo_sem, kv_send, kv_recv, q_send, q_recv, s_send, s_recv, p_send, p_recv,
 ):
     rows, heads, width = ql_ref.shape
@@ -188,8 +188,6 @@
             limit = jnp.where(page == table_ref[r, j], len_ref[r] - j * page_len, limit)
         live.append(offset < limit)
 
-    swap.wait_recv()
-    keys = kv[...].reshape(tokens, key_width)
     block = rows * heads
     for group in GROUPS:
         for e in group:
@@ -197,12 +195,20 @@
                 query_copy(e).wait_recv()
         first, count = group[0], len(group)
         query = qall[first : first + count].reshape(count * block, width + LANES)[:, :key_width]
-        scores = (
-            lax.dot_general(
-                query, keys, (((1,), (1,)), ((), ())), preferred_element_type=jnp.float32
+        halves = []
+        for i in range(2):
+            if i and group == GROUPS[0]:
+                swap.wait_recv()
+            halves.append(
+                lax.dot_general(
+                    query,
+                    kv[i].reshape(tokens // 2, key_width),
+                    (((1,), (1,)), ((), ())),
+                    preferred_element_type=jnp.float32,
+                )
             )
-            * scale
-        )
+        scores = jnp.concatenate(halves, axis=1) * scale
+        keys = kv[:, :, :, :width].reshape(tokens, width)
         scores = jnp.concatenate(
             [
                 jnp.where(live[i % rows], scores[i * heads : (i + 1) * heads], jnp.float32(NEG))
@@ -213,7 +219,7 @@
         top = jnp.max(scores, axis=1, keepdims=True)
         weights = jnp.exp(scores - jnp.maximum(top, jnp.float32(FLOOR))).astype(jnp.bfloat16)
         total = jnp.sum(weights.astype(jnp.float32), axis=1, keepdims=True)
-        summed = jnp.dot(weights, keys[:, :width], preferred_element_type=jnp.float32)
+        summed = jnp.dot(weights, keys, preferred_element_type=jnp.float32)
         states[first : first + count, :, :, :width] = summed.astype(jnp.bfloat16).reshape(
             count, rows, heads, width
         )
@@ -261,16 +267,14 @@
                 ]
     head_out = flat[...].astype(jnp.bfloat16)
 
-    def step(j, carry):
-        load_wo(j).wait()
-        term = jnp.dot(head_out, wo[j], preferred_element_type=jnp.float32)
-        for c in range(TILE // LANES):
-            dense[c * rows : (c + 1) * rows, :] = term[:, c * LANES : (c + 1) * LANES]
-        part[j] = dense[...].astype(jnp.bfloat16)
-        return carry
-
     for begin, end in ((0, tiles - LATE), (tiles - LATE, tiles)):
-        lax.fori_loop(begin, end, step, 0)
+        for j in range(begin, end):
+            load_wo(j).wait()
+            term = jnp.dot(head_out, wo[j], preferred_element_type=jnp.float32)
+            dense = jnp.concatenate(
+                [term[:, c * LANES : (c + 1) * LANES] for c in range(TILE // LANES)], axis=0
+            )
+            part[j] = dense.astype(jnp.bfloat16)
         some = pl.ds(begin, end - begin)
         for k in SEND_ORDER:
             remote(part.at[some], parts.at[k, some], p_send.at[k], p_recv.at[k], k).start()
@@ -319,7 +323,6 @@
             pltpu.VMEM((tiles, dense_rows, LANES), bf16),
             pltpu.VMEM((N, tiles, dense_rows, LANES), bf16),
             pltpu.VMEM((rows, depth), jnp.float32),
-            pltpu.VMEM((dense_rows, LANES), jnp.float32),
             pltpu.SMEM(page_table.shape, jnp.int32),
             pltpu.SMEM(lengths.shape, jnp.int32),
             pltpu.SemaphoreType.DMA((6,)),

time: 22.5 us -> 25.2 us (1.12)
  Pallas kernels: 21.7 us -> 24.4 us
    pallas_call x1, Pallas kernels: 21.7 us -> 24.4 us  [fused(): pl.pallas_call(kernel, out_shape=pltpu.VMEM((rows, columns), jnp.float32)...]
where the time goes in v4:
time: 25.2 us; the launch traced here: 25.1 us
  Pallas kernels  24.4 us (97%)
  other arithmetic  0.63 us (2%)
    pallas_call x1, Pallas kernels, fused(): pl.pallas_call(kernel, out_shape=pltpu.VMEM((rows, columns), jnp.float32)...  24.4 us
    convert_element_type x1, other arithmetic, fused(): return out.astype(bf16)  0.63 us

profile of v4, /device:TPU:0, one launch (start us, length us, event | category | flops | bytes accessed | tf_op | source)
XLA Modules:
  0.0 25.1 jit_solution(6974002180869628335)
XLA Ops:
  0.0 24.4 %shard_map.73 = f32[2,7168]{1,0:T(2,128)S(1)} custom-call(bf16[2,16,512]{2,1,0:T(8,128)(2,1)} %ql_ref.1, bf16[2,16,64]{2,1,0:T(8,128)(2,1)} %qr_ref.1, bf16[8,64,576]{2,1,0:T(8,128)(2,1)} %cache_ref.1, s32[2,32]{1,0:T(2,128)} %table_hbm.1, s32[2]{0:T(128)} %len_hbm.1, bf16[16,512,128]{2,1,0:T(8,128)(2,1)} %uv_ref.1, bf16[2048,7168]{1,0:T(8,128)(2,1)} %wo_ref.1), custom_call_target="tpu_custom_call" | custom-call | flops 58720256 | bytes 29360128 | tf_op jit(solution)/shard_map/pallas_call | solution.py:310
  24.4 0.6 %convert_element_type.3 = bf16[2,7168]{1,0:T(2,128)(2,1)} convert(f32[2,7168]{1,0:T(2,128)S(1)} %shard_map.73) | non-fusion elementwise | flops 14336 | bytes 86016 | tf_op jit(solution)/shard_map/convert_element_type | solution.py:346

commit v5 on v4

--- a/solution.py
+++ b/solution.py
@@ -18,7 +18,6 @@
 LANES = 128
 CHIPS = 4
 GROUPS = ((1, 2, 3), (0,))
-EARLY = 3
 LATE = 2
 CHIP_ORDER = (3, 1, 2)
 SEND_ORDER = (6, 7, 2, 4, 3, 5, 1)
@@ -111,7 +110,7 @@
 
 def kernel(
     ql_ref, qr_ref, cache_ref, table_hbm, len_hbm, uv_ref, wo_ref, out_ref,
-    qall, rope, kv, states, got, uv, wo, part, parts, flat, table_ref, len_ref,
+    qall, rope, kv, states, got, uv, wo, part, parts, flat, dense, table_ref, len_ref,
     local_sem, wo_sem, kv_send, kv_recv, q_send, q_recv, s_send, s_recv, p_send, p_recv,
 ):
     rows, heads, width = ql_ref.shape
@@ -146,9 +145,6 @@
             wo_ref.at[:, pl.ds(pl.multiple_of(j * TILE, TILE), TILE)], wo.at[j], wo_sem.at[j]
         )
 
-    for j in range(EARLY):
-        load_wo(j).start()
-
     def remote(src, dst, send, recv, k):
         return pltpu.make_async_remote_copy(
             src_ref=src, dst_ref=dst, send_sem=send, recv_sem=recv,
@@ -172,7 +168,7 @@
     for e in CHIP_ORDER:
         query_copy(e).start()
     load_uv.start()
-    for j in range(EARLY, tiles):
+    for j in range(tiles):
         load_wo(j).start()
 
     load_table.wait()
@@ -267,14 +263,16 @@
                 ]
     head_out = flat[...].astype(jnp.bfloat16)
 
+    def step(j, carry):
+        load_wo(j).wait()
+        term = jnp.dot(head_out, wo[j], preferred_element_type=jnp.float32)
+        for c in range(TILE // LANES):
+            dense[c * rows : (c + 1) * rows, :] = term[:, c * LANES : (c + 1) * LANES]
+        part[j] = dense[...].astype(jnp.bfloat16)
+        return carry
+
     for begin, end in ((0, tiles - LATE), (tiles - LATE, tiles)):
-        for j in range(begin, end):
-            load_wo(j).wait()
-            term = jnp.dot(head_out, wo[j], preferred_element_type=jnp.float32)
-            dense = jnp.concatenate(
-                [term[:, c * LANES : (c + 1) * LANES] for c in range(TILE // LANES)], axis=0
-            )
-            part[j] = dense.astype(jnp.bfloat16)
+        lax.fori_loop(begin, end, step, 0)
         some = pl.ds(begin, end - begin)
         for k in SEND_ORDER:
             remote(part.at[some], parts.at[k, some], p_send.at[k], p_recv.at[k], k).start()
@@ -323,6 +321,7 @@
             pltpu.VMEM((tiles, dense_rows, LANES), bf16),
             pltpu.VMEM((N, tiles, dense_rows, LANES), bf16),
             pltpu.VMEM((rows, depth), jnp.float32),
+            pltpu.VMEM((dense_rows, LANES), jnp.float32),
             pltpu.SMEM(page_table.shape, jnp.int32),
             pltpu.SMEM(lengths.shape, jnp.int32),
             pltpu.SemaphoreType.DMA((6,)),

time: 25.2 us -> 23.2 us (0.921)
  Pallas kernels: 24.4 us -> 22.4 us
    pallas_call x1, Pallas kernels: 24.4 us -> 22.4 us  [fused(): pl.pallas_call(kernel, out_shape=pltpu.VMEM((rows, columns), jnp.float32)...]
where the time goes in v5:
time: 23.2 us; the launch traced here: 23 us
  Pallas kernels  22.4 us (97%)
  other arithmetic  0.63 us (3%)
    pallas_call x1, Pallas kernels, fused(): pl.pallas_call(kernel, out_shape=pltpu.VMEM((rows, columns), jnp.float32)...  22.4 us
    convert_element_type x1, other arithmetic, fused(): return out.astype(bf16)  0.63 us

profile of v5, /device:TPU:0, one launch (start us, length us, event | category | flops | bytes accessed | tf_op | source)
XLA Modules:
  0.0 23.0 jit_solution(7324900270972097513)
XLA Ops:
  0.0 22.4 %shard_map.73 = f32[2,7168]{1,0:T(2,128)S(1)} custom-call(bf16[2,16,512]{2,1,0:T(8,128)(2,1)} %ql_ref.1, bf16[2,16,64]{2,1,0:T(8,128)(2,1)} %qr_ref.1, bf16[8,64,576]{2,1,0:T(8,128)(2,1)} %cache_ref.1, s32[2,32]{1,0:T(2,128)} %table_hbm.1, s32[2]{0:T(128)} %len_hbm.1, bf16[16,512,128]{2,1,0:T(8,128)(2,1)} %uv_ref.1, bf16[2048,7168]{1,0:T(8,128)(2,1)} %wo_ref.1), custom_call_target="tpu_custom_call" | custom-call | flops 58720256 | bytes 29360128 | tf_op jit(solution)/shard_map/pallas_call | solution.py:308
  22.4 0.6 %convert_element_type.3 = bf16[2,7168]{1,0:T(2,128)(2,1)} convert(f32[2,7168]{1,0:T(2,128)S(1)} %shard_map.73) | non-fusion elementwise | flops 14336 | bytes 86016 | tf_op jit(solution)/shard_map/convert_element_type | solution.py:345

commit v6 on v3

--- a/solution.py
+++ b/solution.py
@@ -18,7 +18,7 @@
 LANES = 128
 CHIPS = 4
 GROUPS = ((1, 2, 3), (0,))
-EARLY = 1
+EARLY = 2
 LATE = 2
 CHIP_ORDER = (3, 1, 2)
 SEND_ORDER = (6, 7, 2, 4, 3, 5, 1)
@@ -146,9 +146,6 @@
             wo_ref.at[:, pl.ds(pl.multiple_of(j * TILE, TILE), TILE)], wo.at[j], wo_sem.at[j]
         )
 
-    for j in range(EARLY):
-        load_wo(j).start()
-
     def remote(src, dst, send, recv, k):
         return pltpu.make_async_remote_copy(
             src_ref=src, dst_ref=dst, send_sem=send, recv_sem=recv,
@@ -171,8 +168,7 @@
     swap.start()
     for e in CHIP_ORDER:
         query_copy(e).start()
-    load_uv.start()
-    for j in range(EARLY, tiles):
+    for j in range(EARLY):
         load_wo(j).start()
 
     load_table.wait()
@@ -227,6 +223,10 @@
         for e in group:
             if e:
                 state_copy(e).start()
+        if group == GROUPS[0]:
+            load_uv.start()
+            for j in range(EARLY, tiles):
+                load_wo(j).start()
 
     place = lax.broadcasted_iota(jnp.int32, (block, LANES), 1)
     tops, sums = [], []

time: 22.5 us -> 25.8 us (1.15)
  Pallas kernels: 21.7 us -> 25 us
    pallas_call x1, Pallas kernels: 21.7 us -> 25 us  [fused(): pl.pallas_call(kernel, out_shape=pltpu.VMEM((rows, columns), jnp.float32)...]
where the time goes in v6:
time: 25.8 us; the launch traced here: 25.6 us
  Pallas kernels  25 us (97%)
  other arithmetic  0.63 us (2%)
    pallas_call x1, Pallas kernels, fused(): pl.pallas_call(kernel, out_shape=pltpu.VMEM((rows, columns), jnp.float32)...  25 us
    convert_element_type x1, other arithmetic, fused(): return out.astype(bf16)  0.63 us

profile of v6, /device:TPU:0, one launch (start us, length us, event | category | flops | bytes accessed | tf_op | source)
XLA Modules:
  0.0 25.6 jit_solution(10976878932142928312)
XLA Ops:
  0.0 25.0 %shard_map.73 = f32[2,7168]{1,0:T(2,128)S(1)} custom-call(bf16[2,16,512]{2,1,0:T(8,128)(2,1)} %ql_ref.1, bf16[2,16,64]{2,1,0:T(8,128)(2,1)} %qr_ref.1, bf16[8,64,576]{2,1,0:T(8,128)(2,1)} %cache_ref.1, s32[2,32]{1,0:T(2,128)} %table_hbm.1, s32[2]{0:T(128)} %len_hbm.1, bf16[16,512,128]{2,1,0:T(8,128)(2,1)} %uv_ref.1, bf16[2048,7168]{1,0:T(8,128)(2,1)} %wo_ref.1), custom_call_target="tpu_custom_call" | custom-call | flops 58720256 | bytes 29360128 | tf_op jit(solution)/shard_map/pallas_call | solution.py:306
  25.0 0.6 %convert_element_type.3 = bf16[2,7168]{1,0:T(2,128)(2,1)} convert(f32[2,7168]{1,0:T(2,128)S(1)} %shard_map.73) | non-fusion elementwise | flops 14336 | bytes 86016 | tf_op jit(solution)/shard_map/convert_element_type | solution.py:343
